TPU v7x, 512 devices: a whole 4x8x8 slice. The times are simulated.
512 devices in a mesh: grp: 8 (over y_lo, core), tile: 64 (over y_hi, x, z).
Axes of the slice: x: 4, y: 8 (y_hi: 2, y_lo: 4; y = y_hi * 4 + y_lo), z: 8, core: 2. Of those that a mesh axis runs over, the one named last changes fastest.
Arguments:
- hidden: bfloat16 [8, 512, 128, 128], P('grp', 'tile'), may hold values from -13 to 13
- cotangent: float32 [8, 512, 128], P('grp', 'tile'), may hold values from -16 to 16
- spectral_w: bfloat16 [4096, 256], P('tile'), may hold values from -0.375 to 0.375
- conv_k: float32 [9, 128], replicated, may hold values from -2 to 2
- proj_w: float32 [128], replicated, may hold values from -0.5 to 0.5
Outputs:
- grad_hidden: float32 [8, 512, 128, 128], P('grp', 'tile')
- grad_spectral: float32 [4096, 256], P('tile')
- grad_conv: float32 [9, 128], replicated
- grad_proj: float32 [128], replicated
All inputs are finite; a program needn't handle non-finite values.
Results may differ from a plain program's by a relative error of at most 0.015.
Values may be sent and summed in bfloat16 or wider, within the bound.
No kernel may reach another device: no remote copies, remote signals or barrier semaphores. Data moves between devices by JAX's collectives and lax.ppermute only.
A program may use at most 64 MiB of HBM per device.

v0:
```python
import jax
import jax.numpy as jnp
from jax import lax
from jax.sharding import PartitionSpec as P

HIGH = lax.Precision.HIGHEST


def padded(block, sides, width):
    for axis, dim in sides:
        count = lax.axis_size(axis)
        forward = [(i, i + 1) for i in range(count - 1)]
        backward = [(target, source) for source, target in forward]
        low = lax.ppermute(
            lax.slice_in_dim(block, block.shape[dim] - width, None, axis=dim), axis, forward
        )
        high = lax.ppermute(lax.slice_in_dim(block, 0, width, axis=dim), axis, backward)
        block = jnp.concatenate([low, block, high], axis=dim)
    return block


def spectral_tables(modes, bins):
    mode_idx = jnp.arange(modes, dtype=jnp.int32)
    bin_idx = jnp.arange(bins, dtype=jnp.int32)
    phase_int = mode_idx[:, None] * bin_idx[None, :] % bins
    angle_val = phase_int.astype(jnp.float32) * (2.0 * jnp.pi / bins)
    cosine = jnp.cos(angle_val)
    sine = jnp.sin(angle_val)
    forward_tab = jnp.concatenate([cosine, -sine], 0).astype(jnp.bfloat16)
    weight_k = jnp.where(mode_idx == 0, 1.0, 2.0).astype(jnp.float32)[:, None] / bins
    inverse_tab = jnp.concatenate([cosine * weight_k, -sine * weight_k], 0).T.astype(jnp.bfloat16)
    return (forward_tab, inverse_tab)


def build_mixer(weights, modes, chans):
    real_w = weights[:, :chans].reshape(modes, chans, chans)
    imag_w = weights[:, chans:].reshape(modes, chans, chans)
    upper = jnp.concatenate([real_w, imag_w], 2)
    lower = jnp.concatenate([-imag_w, real_w], 2)
    return jnp.concatenate([upper, lower], 1)


def gelu_pair(value):
    normal_cdf = 0.5 * (1.0 + jax.scipy.special.erf(value * 0.7071067811865476))
    return (
        value * normal_cdf,
        normal_cdf + value * jnp.exp(-0.5 * value * value) * 0.3989422804014327,
    )


def cell_backward(hidden_cells, local_term, cot_cells, mixer, forward_tab, inverse_tab, proj_w):
    modes = mixer.shape[0]
    chans = proj_w.shape[0]
    spec_h = jnp.einsum(
        "jb,pbc->jpc", forward_tab, hidden_cells, preferred_element_type=jnp.float32
    ).astype(jnp.bfloat16)
    h_cat = jnp.concatenate([spec_h[:modes], spec_h[modes:]], 2)
    mixed = jnp.einsum("kpa,kab->kpb", h_cat, mixer, preferred_element_type=jnp.float32).astype(
        jnp.bfloat16
    )
    mixed_stack = jnp.concatenate([mixed[:, :, :chans], mixed[:, :, chans:]], 0)
    spectral_out = jnp.einsum(
        "bj,jpo->pbo", inverse_tab, mixed_stack, preferred_element_type=jnp.float32
    )
    pre_act = spectral_out + local_term
    activ, slope = gelu_pair(pre_act)
    proj_grad = jnp.einsum("pb,pbo->o", cot_cells, activ, precision=HIGH)
    grad_pre = (cot_cells[:, :, None] * proj_w * slope).astype(jnp.bfloat16)
    grad_mix = jnp.einsum(
        "bj,pbo->jpo", inverse_tab, grad_pre, preferred_element_type=jnp.float32
    ).astype(jnp.bfloat16)
    grad_real = grad_mix[:modes]
    grad_imag = grad_mix[modes:]
    grad_cat = jnp.concatenate([grad_real, grad_imag], 2)
    grad_spec = jnp.einsum(
        "kpb,kab->kpa", grad_cat, mixer, preferred_element_type=jnp.float32
    ).astype(jnp.bfloat16)
    grad_stack = jnp.concatenate([grad_spec[:, :, :chans], grad_spec[:, :, chans:]], 0)
    grad_in = jnp.einsum("jb,jpc->pbc", forward_tab, grad_stack, preferred_element_type=jnp.float32)
    left_side = jnp.concatenate([spec_h[:modes], spec_h[modes:]], 1)
    right_side = jnp.concatenate([grad_cat, jnp.concatenate([grad_imag, -grad_real], 2)], 1)
    weight_term = jnp.einsum(
        "kpc,kpo->kco", left_side, right_side, preferred_element_type=jnp.float32
    ).reshape(modes * chans, 2 * chans)
    return (grad_pre, grad_in, weight_term, proj_grad)


def local(hidden, cotangent, spectral_w, conv_k, proj_w):
    rows_here, cols_here, bins_here, chans = hidden.shape
    modes = spectral_w.shape[0] * lax.axis_size("tile") // chans
    cell_count = rows_here * cols_here
    forward_tab, inverse_tab = spectral_tables(modes, bins_here)
    x_pad = padded(hidden, (("grp", 0), ("tile", 1)), 1)
    offsets = [(row_off, col_off) for row_off in (-1, 0, 1) for col_off in (-1, 0, 1)]
    local_term = jnp.zeros((rows_here, cols_here, bins_here, chans), jnp.float32)
    for index_d, (row_off, col_off) in enumerate(offsets):
        window = x_pad[1 + row_off : 1 + row_off + rows_here, 1 + col_off : 1 + col_off + cols_here]
        local_term = local_term + window.astype(jnp.float32) * conv_k[index_d]
    whole_w = lax.all_gather(spectral_w, "tile", axis=0, tiled=True)
    mixer = build_mixer(whole_w, modes, chans)
    grad_pre, grad_in, weight_term, proj_grad = cell_backward(
        hidden.reshape(cell_count, bins_here, chans),
        local_term.reshape(cell_count, bins_here, chans),
        cotangent.reshape(cell_count, bins_here),
        mixer,
        forward_tab,
        inverse_tab,
        proj_w,
    )
    grad_block = grad_pre.reshape(rows_here, cols_here, bins_here, chans)
    conv_part = jnp.stack(
        [
            jnp.einsum(
                "xybc,xybc->c",
                x_pad[1 + row_off : 1 + row_off + rows_here, 1 + col_off : 1 + col_off + cols_here],
                grad_block,
                preferred_element_type=jnp.float32,
            )
            for row_off, col_off in offsets
        ],
        0,
    )
    grad_pad = padded(grad_block, (("grp", 0), ("tile", 1)), 1)
    grad_hidden = grad_in.reshape(rows_here, cols_here, bins_here, chans)
    for index_d, (row_off, col_off) in enumerate(offsets):
        window = grad_pad[
            1 - row_off : 1 - row_off + rows_here, 1 - col_off : 1 - col_off + cols_here
        ]
        grad_hidden = grad_hidden + window.astype(jnp.float32) * conv_k[index_d]
    tile_share = lax.psum_scatter(weight_term, "tile", scatter_dimension=0, tiled=True)
    grad_spectral = lax.psum(tile_share.astype(jnp.bfloat16), "grp").astype(jnp.float32)
    conv_all, proj_all = lax.psum((conv_part, proj_grad), ("grp", "tile"))
    return (grad_hidden, grad_spectral, conv_all, proj_all)


def solution(mesh):
    in_specs = (P("grp", "tile", None, None), P("grp", "tile", None), P("tile", None), P(), P())
    out_specs = (P("grp", "tile", None, None), P("tile", None), P(), P())
    return jax.shard_map(local, mesh=mesh, in_specs=in_specs, out_specs=out_specs, check_vma=False)
```

profile of v0, /device:TPU:1, one launch (start us, length us, event | category | flops | bytes accessed | tf_op | source)
XLA Modules:
  0.0 639.4 jit_solution(11236863667525213482)
XLA Ops:
  7.2 0.7 all-gather.2.cloned.1.call-update
  7.9 1.1 copy.11
  9.1 8.8 %collective-permute-start.1 = (bf16[1,8,128,128]{2,3,1,0:T(8,128)(2,1)S(1)}, bf16[1,8,128,128]{2,3,1,0:T(8,128)(2,1)S(1)}, u32[]{:S(2)}, u32[]{:S(2)}) collective-permute-start(bf16[1,8,128,128]{2,3,1,0:T(8,128)(2,1)S(1)} %copy.11), channel_id=1, source_target_pairs={{64,0},{128,64},{192,128},{256,192},{320,256},{384,320},{448,384},... | collective-permute-start | bytes 786440 | tf_op jit(solution)/shard_map/ppermute | solution.py:17
  17.9 1.9 collective-permute-start
  19.9 1.1 convolution_convert_fusion.1
  21.1 1.0 slice_bitcast_fusion.8
  22.3 0.8 collective-permute-done
  23.1 1.3 collective-permute-start.3
  24.4 4.0 collective-permute-start.2
  28.4 119.3 %all-gather.2.cloned.1.call-done = bf16[4096,256]{1,0:T(8,128)(2,1)} async-done(((bf16[64,256]{1,0:T(8,128)(2,1)}), bf16[4096,256]{1,0:T(8,128)(2,1)}) %all-gather.2.cloned.1.call-update) | async-done | bytes 2097168 | tf_op jit(solution)/shard_map/all_gather | solution.py:99
  147.7 1.7 fusion.52
  149.7 0.9 fusion.2
  150.9 1.6 bitcast_convert_fusion
  152.8 2.7 fusion.24
  155.5 6.4 %collective-permute-start.5 = (bf16[1,8,128,128]{2,3,1,0:T(8,128)(2,1)S(1)}, bf16[1,8,128,128]{2,3,1,0:T(8,128)(2,1)}, u32[]{:S(2)}, u32[]{:S(2)}) collective-permute-start(bf16[1,8,128,128]{2,3,1,0:T(8,128)(2,1)S(1)} %bitcast.128), channel_id=1, source_target_pairs={{64,0},{128,64},{192,128},{256,192},{320,256},{384,320},{448,384},... | collective-permute-start | bytes 786440 | tf_op jit(solution)/shard_map/ppermute | solution.py:17
  161.9 5.1 collective-permute-start.4
  167.4 1.0 fusion.14
  168.4 1.2 fusion.15
  169.7 3.2 fusion.3
  172.9 0.6 convolution_bitcast_fusion.2
  173.5 97.4 %all-reduce = (f32[9,128]{1,0:T(8,128)}, f32[128]{0:T(128)}) all-reduce(f32[9,128]{1,0:T(8,128)S(1)} %stack.39, f32[128]{0:T(128)S(1)} %convolution_bitcast_fusion.2), channel_id=1, replica_groups=mesh['grp'=8,'tile'=64] {'grp','tile'}, use_global_device_ids=true, to_apply=%region_2.3 | all-reduce | flops 1280 | bytes 10240 | tf_op jit(solution)/shard_map/psum | solution.py:132
  270.9 0.8 pad_maximum_fusion.23
  271.8 1.3 collective-permute-start.6
  273.1 4.0 collective-permute-start.7
  277.1 0.4 collective-permute-done.6
  277.5 1.3 collective-permute-done.7
  278.9 2.1 fusion.21
  281.1 1.0 copy.20
  282.1 273.8 %reduce-scatter.2.cloned.1.call-done = f32[64,256]{1,0:T(8,128)} async-done(((f32[4096,256]{1,0:T(8,128)}), f32[64,256]{1,0:T(8,128)}) %reduce-scatter.2.cloned.1.call-update) | async-done | bytes 65552 | tf_op jit(solution)/shard_map/reduce_scatter | solution.py:130
  555.8 0.8 convert_element_type.112
  556.7 75.3 %psum.21 = bf16[64,256]{1,0:T(8,128)(2,1)S(1)} all-reduce(bf16[64,256]{1,0:T(8,128)(2,1)S(1)} %convert_element_type.112), channel_id=1, replica_groups=mesh['grp'=8,'tile'=64] {'grp'}, use_global_device_ids=true, to_apply=%region_1.2 | all-reduce | flops 16384 | bytes 65536 | tf_op jit(solution)/shard_map/psum | solution.py:131
  632.0 0.6 convert_element_type.113
  (81 shorter events, 1.6 us)
Async XLA Ops:
  7.2 140.5 %all-gather.2.cloned.1.call-start = ((), (), s32[]{:S(2)}) async-start(), calls=%async_computation.1 | async-start | bytes 2129920 | tf_op jit(solution)/shard_map/all_gather | solution.py:99
  7.9 548.0 %reduce-scatter.2.cloned.1.call-start = ((), (), s32[]{:S(2)}) async-start(), calls=%async_computation.2 | async-start | bytes 4259840 | tf_op jit(solution)/shard_map/reduce_scatter | solution.py:130
  9.1 13.2 %collective-permute-start.1 = (bf16[1,8,128,128]{2,3,1,0:T(8,128)(2,1)S(1)}, bf16[1,8,128,128]{2,3,1,0:T(8,128)(2,1)S(1)}, u32[]{:S(2)}, u32[]{:S(2)}) collective-permute-start(bf16[1,8,128,128]{2,3,1,0:T(8,128)(2,1)S(1)} %copy.11), channel_id=1, source_target_pairs={{64,0},{128,64},{192,128},{256,192},{320,256},{384,320},{448,384},... | collective-permute-start | bytes 786440 | tf_op jit(solution)/shard_map/ppermute | solution.py:17
  17.9 5.2 collective-permute-start
  22.1 128.7 %copy-start.5 = (f32[128]{0:T(128)}, f32[128]{0:T(128)S(1)}, u32[]{:S(2)}) copy-start(f32[128]{0:T(128)S(1)} %get-tuple-element.35) | copy-start | bytes 1540
  22.1 128.7 %copy-start.7 = (f32[128]{0:T(128)}, f32[128]{0:T(128)S(1)}, u32[]{:S(2)}) copy-start(f32[128]{0:T(128)S(1)} %get-tuple-element.36) | copy-start | bytes 1540
  22.1 128.7 %copy-start.9 = (f32[128]{0:T(128)}, f32[128]{0:T(128)S(1)}, u32[]{:S(2)}) copy-start(f32[128]{0:T(128)S(1)} %get-tuple-element.37) | copy-start | bytes 1540
  22.1 128.7 %copy-start.11 = (f32[128]{0:T(128)}, f32[128]{0:T(128)S(1)}, u32[]{:S(2)}) copy-start(f32[128]{0:T(128)S(1)} %get-tuple-element.38) | copy-start | bytes 1540
  22.1 128.7 %copy-start.13 = (f32[128]{0:T(128)}, f32[128]{0:T(128)S(1)}, u32[]{:S(2)}) copy-start(f32[128]{0:T(128)S(1)} %get-tuple-element.39) | copy-start | bytes 1540
  22.1 128.7 %copy-start.15 = (f32[128]{0:T(128)}, f32[128]{0:T(128)S(1)}, u32[]{:S(2)}) copy-start(f32[128]{0:T(128)S(1)} %get-tuple-element.40) | copy-start | bytes 1540
  22.1 128.7 %copy-start.17 = (f32[128]{0:T(128)}, f32[128]{0:T(128)S(1)}, u32[]{:S(2)}) copy-start(f32[128]{0:T(128)S(1)} %get-tuple-element.41) | copy-start | bytes 1540
  22.1 128.7 %copy-start.19 = (f32[128]{0:T(128)}, f32[128]{0:T(128)S(1)}, u32[]{:S(2)}) copy-start(f32[128]{0:T(128)S(1)} %get-tuple-element.42) | copy-start | bytes 1540
  22.2 128.7 %copy-start.21 = (f32[128]{0:T(128)}, f32[128]{0:T(128)S(1)}, u32[]{:S(2)}) copy-start(f32[128]{0:T(128)S(1)} %get-tuple-element.43) | copy-start | bytes 1540
  23.1 127.7 %collective-permute-start.3 = (bf16[3,1,128,128]{2,3,1,0:T(8,128)(2,1)S(1)}, bf16[3,1,128,128]{2,3,1,0:T(8,128)(2,1)S(1)}, u32[]{:S(2)}, u32[]{:S(2)}) collective-permute-start(bf16[3,1,128,128]{2,3,1,0:T(8,128)(2,1)S(1)} %get-tuple-element.24), channel_id=1, source_target_pairs={{1,0},{2,1},{3,2},{4,3},{5,4},{6,5},{7,6},{8,7},{9,8},{10,9},{11,1... | collective-permute-start | bytes 294920 | tf_op jit(solution)/shard_map/ppermute | solution.py:17
  24.4 126.4 %collective-permute-start.2 = (bf16[3,1,128,128]{2,3,1,0:T(8,128)(2,1)S(1)}, bf16[3,1,128,128]{2,3,1,0:T(8,128)(2,1)S(1)}, u32[]{:S(2)}, u32[]{:S(2)}) collective-permute-start(bf16[3,1,128,128]{2,3,1,0:T(8,128)(2,1)S(1)} %get-tuple-element.25), channel_id=1, source_target_pairs={{0,1},{1,2},{2,3},{3,4},{4,5},{5,6},{6,7},{7,8},{8,9},{9,10},{10,1... | collective-permute-start | bytes 294920 | tf_op jit(solution)/shard_map/ppermute | solution.py:14
  150.8 1.7 copy-start.3
  152.8 14.5 %copy-start = (bf16[1,8,128,128]{3,2,1,0:T(8,128)(2,1)S(1)}, bf16[1,8,128,128]{3,2,1,0:T(8,128)(2,1)}, u32[]{:S(2)}) copy-start(bf16[1,8,128,128]{3,2,1,0:T(8,128)(2,1)} %param.5) | copy-start | bytes 786436
  155.5 115.4 %collective-permute-start.5 = (bf16[1,8,128,128]{2,3,1,0:T(8,128)(2,1)S(1)}, bf16[1,8,128,128]{2,3,1,0:T(8,128)(2,1)}, u32[]{:S(2)}, u32[]{:S(2)}) collective-permute-start(bf16[1,8,128,128]{2,3,1,0:T(8,128)(2,1)S(1)} %bitcast.128), channel_id=1, source_target_pairs={{64,0},{128,64},{192,128},{256,192},{320,256},{384,320},{448,384},... | collective-permute-start | bytes 786440 | tf_op jit(solution)/shard_map/ppermute | solution.py:17
  161.9 109.0 %collective-permute-start.4 = (bf16[1,8,128,128]{2,3,1,0:T(8,128)(2,1)S(1)}, bf16[1,8,128,128]{2,3,1,0:T(8,128)(2,1)}, u32[]{:S(2)}, u32[]{:S(2)}) collective-permute-start(bf16[1,8,128,128]{2,3,1,0:T(8,128)(2,1)S(1)} %bitcast.129), channel_id=1, source_target_pairs={{0,64},{64,128},{128,192},{192,256},{256,320},{320,384},{384,448},... | collective-permute-start | bytes 786440 | tf_op jit(solution)/shard_map/ppermute | solution.py:14
  169.6 3.3 copy-start.24
  169.6 3.3 copy-start.26
  169.6 109.2 %copy-start.6 = (f32[128]{0:T(128)S(1)}, f32[128]{0:T(128)}, u32[]{:S(2)}) copy-start(f32[128]{0:T(128)} %copy-done.5) | copy-start | bytes 1540
  169.6 109.2 %copy-start.8 = (f32[128]{0:T(128)S(1)}, f32[128]{0:T(128)}, u32[]{:S(2)}) copy-start(f32[128]{0:T(128)} %copy-done.7) | copy-start | bytes 1540
  169.6 109.2 %copy-start.10 = (f32[128]{0:T(128)S(1)}, f32[128]{0:T(128)}, u32[]{:S(2)}) copy-start(f32[128]{0:T(128)} %copy-done.9) | copy-start | bytes 1540
  169.6 109.2 %copy-start.12 = (f32[128]{0:T(128)S(1)}, f32[128]{0:T(128)}, u32[]{:S(2)}) copy-start(f32[128]{0:T(128)} %copy-done.11) | copy-start | bytes 1540
  169.7 109.2 %copy-start.14 = (f32[128]{0:T(128)S(1)}, f32[128]{0:T(128)}, u32[]{:S(2)}) copy-start(f32[128]{0:T(128)} %copy-done.13) | copy-start | bytes 1540
  169.7 109.2 %copy-start.16 = (f32[128]{0:T(128)S(1)}, f32[128]{0:T(128)}, u32[]{:S(2)}) copy-start(f32[128]{0:T(128)} %copy-done.15) | copy-start | bytes 1540
  169.7 109.2 %copy-start.18 = (f32[128]{0:T(128)S(1)}, f32[128]{0:T(128)}, u32[]{:S(2)}) copy-start(f32[128]{0:T(128)} %copy-done.17) | copy-start | bytes 1540
  169.7 109.2 %copy-start.20 = (f32[128]{0:T(128)S(1)}, f32[128]{0:T(128)}, u32[]{:S(2)}) copy-start(f32[128]{0:T(128)} %copy-done.19) | copy-start | bytes 1540
  169.7 109.2 %copy-start.22 = (f32[128]{0:T(128)S(1)}, f32[128]{0:T(128)}, u32[]{:S(2)}) copy-start(f32[128]{0:T(128)} %copy-done.21) | copy-start | bytes 1540
  271.8 5.8 collective-permute-start.6
  273.1 5.8 collective-permute-start.7
  (5 other events, 6.4 us)
Sparse Core Ops, SparseCore 0:
  12.6 135.0 all-gather.1
  155.6 400.1 reduce-scatter.1
where the time goes:
time: 640 us; the launch traced here: 639 us
  waiting for transfers between devices  396 us (62%)
  blocking collectives  173 us (27%)
  starting transfers between devices  32.8 us (5%)
  between operations  14.6 us (2%)
  matrix products  12.4 us (2%)
    reduce_scatter x1, waiting for transfers between devices, local(): lax.psum_scatter(weight_term, 'tile', scatter_dimension=0, tiled=True)  274 us
    all_gather x1, waiting for transfers between devices, local(): whole_w = lax.all_gather(spectral_w, 'tile', axis=0, tiled=True)  119 us
    psum x1, blocking collectives, local(): conv_all, proj_all = lax.psum((conv_part, proj_grad), ('grp', 'tile'))  97.4 us
    psum x1, blocking collectives, local(): lax.psum(tile_share.astype(jnp.bfloat16), 'grp').astype(jnp.float32)  75.3 us
    ppermute x4, starting transfers between devices, padded(): lax.ppermute(lax.slice_in_dim(block, 0, width, axis=dim), axis, backward)  17.8 us
    ppermute x4, starting transfers between devices, padded(): lax.ppermute(lax.slice_in_dim(block, block.shape[dim] - width, None, axis...  15 us
  transfers between devices with their start and end apart: 10, of which 5 were waited for; matrix products, arithmetic and copies ran while one was open for 3% of the time, Pallas kernels for 0%

commit v1 on v0

--- a/solution.py
+++ b/solution.py
@@ -128,7 +128,9 @@
         ]
         grad_hidden = grad_hidden + window.astype(jnp.float32) * conv_k[index_d]
     tile_share = lax.psum_scatter(weight_term, "tile", scatter_dimension=0, tiled=True)
-    grad_spectral = lax.psum(tile_share.astype(jnp.bfloat16), "grp").astype(jnp.float32)
+    grad_spectral = jnp.sum(jax.lax.all_gather(tile_share.astype(jnp.bfloat16), "grp"), 0).astype(
+        jnp.float32
+    )
     conv_all, proj_all = lax.psum((conv_part, proj_grad), ("grp", "tile"))
     return (grad_hidden, grad_spectral, conv_all, proj_all)
 

time: 640 us -> 632 us (0.988)
  blocking collectives: 173 us -> 165 us
    psum x1 -> x0, blocking collectives: 75.3 us -> none  [local(): lax.psum(tile_share.astype(jnp.bfloat16), 'grp').astype(jnp.float32)]
    all_gather x0 -> x1, blocking collectives: none -> 67.4 us  [local(): jax.lax.all_gather(tile_share.astype(jnp.bfloat16), 'grp')]
where the time goes in v1:
time: 632 us
  waiting for transfers between devices  396 us (63%)
  blocking collectives  165 us (26%)
  starting transfers between devices  32.8 us (5%)
  between operations  14.6 us (2%)
  matrix products  12.4 us (2%)
    reduce_scatter x1, waiting for transfers between devices, local(): lax.psum_scatter(weight_term, 'tile', scatter_dimension=0, tiled=True)  274 us
    all_gather x1, waiting for transfers between devices, local(): whole_w = lax.all_gather(spectral_w, 'tile', axis=0, tiled=True)  119 us
    psum x1, blocking collectives, local(): conv_all, proj_all = lax.psum((conv_part, proj_grad), ('grp', 'tile'))  97.4 us
    all_gather x1, blocking collectives, local(): jax.lax.all_gather(tile_share.astype(jnp.bfloat16), 'grp')  67.4 us
    ppermute x4, starting transfers between devices, padded(): lax.ppermute(lax.slice_in_dim(block, 0, width, axis=dim), axis, backward)  17.8 us
    ppermute x4, starting transfers between devices, padded(): lax.ppermute(lax.slice_in_dim(block, block.shape[dim] - width, None, axis...  15 us
  transfers between devices with their start and end apart: 10, of which 5 were waited for; matrix products, arithmetic and copies ran while one was open for 3% of the time, Pallas kernels for 0%

profile of v1, /device:TPU:1, one launch (start us, length us, event | category | flops | bytes accessed | tf_op | source)
XLA Modules:
  0.0 631.7 jit_solution(8318704303405119855)
XLA Ops:
  7.2 0.7 all-gather.3.cloned.1.call-update
  7.9 1.1 copy.11
  9.1 8.8 %collective-permute-start.1 = (bf16[1,8,128,128]{2,3,1,0:T(8,128)(2,1)S(1)}, bf16[1,8,128,128]{2,3,1,0:T(8,128)(2,1)S(1)}, u32[]{:S(2)}, u32[]{:S(2)}) collective-permute-start(bf16[1,8,128,128]{2,3,1,0:T(8,128)(2,1)S(1)} %copy.11), channel_id=1, source_target_pairs={{64,0},{128,64},{192,128},{256,192},{320,256},{384,320},{448,384},... | collective-permute-start | bytes 786440 | tf_op jit(solution)/shard_map/ppermute | solution.py:17
  17.9 1.9 collective-permute-start
  19.9 1.1 convolution_convert_fusion.1
  21.1 1.0 slice_bitcast_fusion.8
  22.3 0.8 collective-permute-done
  23.1 1.3 collective-permute-start.3
  24.4 4.0 collective-permute-start.2
  28.4 119.3 %all-gather.3.cloned.1.call-done = bf16[4096,256]{1,0:T(8,128)(2,1)} async-done(((bf16[64,256]{1,0:T(8,128)(2,1)}), bf16[4096,256]{1,0:T(8,128)(2,1)}) %all-gather.3.cloned.1.call-update) | async-done | bytes 2097168 | tf_op jit(solution)/shard_map/all_gather | solution.py:99
  147.7 1.7 fusion.52
  149.7 0.9 fusion.2
  150.9 1.6 bitcast_convert_fusion
  152.8 2.7 fusion.24
  155.5 6.4 %collective-permute-start.5 = (bf16[1,8,128,128]{2,3,1,0:T(8,128)(2,1)S(1)}, bf16[1,8,128,128]{2,3,1,0:T(8,128)(2,1)}, u32[]{:S(2)}, u32[]{:S(2)}) collective-permute-start(bf16[1,8,128,128]{2,3,1,0:T(8,128)(2,1)S(1)} %bitcast.129), channel_id=1, source_target_pairs={{64,0},{128,64},{192,128},{256,192},{320,256},{384,320},{448,384},... | collective-permute-start | bytes 786440 | tf_op jit(solution)/shard_map/ppermute | solution.py:17
  161.9 5.1 collective-permute-start.4
  167.4 1.0 fusion.14
  168.4 1.2 fusion.15
  169.7 3.2 fusion.3
  172.9 0.6 convolution_bitcast_fusion.2
  173.5 97.4 %all-reduce = (f32[9,128]{1,0:T(8,128)}, f32[128]{0:T(128)}) all-reduce(f32[9,128]{1,0:T(8,128)S(1)} %stack.39, f32[128]{0:T(128)S(1)} %convolution_bitcast_fusion.2), channel_id=1, replica_groups=mesh['grp'=8,'tile'=64] {'grp','tile'}, use_global_device_ids=true, to_apply=%region_2.3 | all-reduce | flops 1280 | bytes 10240 | tf_op jit(solution)/shard_map/psum | solution.py:134
  270.9 0.8 pad_maximum_fusion.23
  271.8 1.3 collective-permute-start.6
  273.1 4.0 collective-permute-start.7
  277.1 0.4 collective-permute-done.6
  277.5 1.3 collective-permute-done.7
  278.9 2.1 fusion.21
  281.1 1.0 copy.20
  282.1 273.8 %reduce-scatter.2.cloned.1.call-done = f32[64,256]{1,0:T(8,128)} async-done(((f32[4096,256]{1,0:T(8,128)}), f32[64,256]{1,0:T(8,128)}) %reduce-scatter.2.cloned.1.call-update) | async-done | bytes 65552 | tf_op jit(solution)/shard_map/reduce_scatter | solution.py:130
  555.8 0.8 convert_element_type.114
  556.7 67.4 %all-gather = bf16[512,256]{1,0:T(8,128)(2,1)S(1)} all-gather(bf16[64,256]{1,0:T(8,128)(2,1)S(1)} %convert_element_type.114), channel_id=2, replica_groups=mesh['grp'=8,'tile'=64] {'grp'}, dimensions={0}, use_global_device_ids=true | all-gather | bytes 294912 | tf_op jit(solution)/shard_map/all_gather | solution.py:131
  624.2 0.6 convert_element_type.115
  (82 shorter events, 1.7 us)
Async XLA Ops:
  7.2 140.5 %all-gather.3.cloned.1.call-start = ((), (), s32[]{:S(2)}) async-start(), calls=%async_computation.1 | async-start | bytes 2129920 | tf_op jit(solution)/shard_map/all_gather | solution.py:99
  7.9 548.0 %reduce-scatter.2.cloned.1.call-start = ((), (), s32[]{:S(2)}) async-start(), calls=%async_computation.2 | async-start | bytes 4259840 | tf_op jit(solution)/shard_map/reduce_scatter | solution.py:130
  9.1 13.2 %collective-permute-start.1 = (bf16[1,8,128,128]{2,3,1,0:T(8,128)(2,1)S(1)}, bf16[1,8,128,128]{2,3,1,0:T(8,128)(2,1)S(1)}, u32[]{:S(2)}, u32[]{:S(2)}) collective-permute-start(bf16[1,8,128,128]{2,3,1,0:T(8,128)(2,1)S(1)} %copy.11), channel_id=1, source_target_pairs={{64,0},{128,64},{192,128},{256,192},{320,256},{384,320},{448,384},... | collective-permute-start | bytes 786440 | tf_op jit(solution)/shard_map/ppermute | solution.py:17
  17.9 5.2 collective-permute-start
  22.1 128.7 %copy-start.5 = (f32[128]{0:T(128)}, f32[128]{0:T(128)S(1)}, u32[]{:S(2)}) copy-start(f32[128]{0:T(128)S(1)} %get-tuple-element.35) | copy-start | bytes 1540
  22.1 128.7 %copy-start.7 = (f32[128]{0:T(128)}, f32[128]{0:T(128)S(1)}, u32[]{:S(2)}) copy-start(f32[128]{0:T(128)S(1)} %get-tuple-element.36) | copy-start | bytes 1540
  22.1 128.7 %copy-start.9 = (f32[128]{0:T(128)}, f32[128]{0:T(128)S(1)}, u32[]{:S(2)}) copy-start(f32[128]{0:T(128)S(1)} %get-tuple-element.37) | copy-start | bytes 1540
  22.1 128.7 %copy-start.11 = (f32[128]{0:T(128)}, f32[128]{0:T(128)S(1)}, u32[]{:S(2)}) copy-start(f32[128]{0:T(128)S(1)} %get-tuple-element.38) | copy-start | bytes 1540
  22.1 128.7 %copy-start.13 = (f32[128]{0:T(128)}, f32[128]{0:T(128)S(1)}, u32[]{:S(2)}) copy-start(f32[128]{0:T(128)S(1)} %get-tuple-element.39) | copy-start | bytes 1540
  22.1 128.7 %copy-start.15 = (f32[128]{0:T(128)}, f32[128]{0:T(128)S(1)}, u32[]{:S(2)}) copy-start(f32[128]{0:T(128)S(1)} %get-tuple-element.40) | copy-start | bytes 1540
  22.1 128.7 %copy-start.17 = (f32[128]{0:T(128)}, f32[128]{0:T(128)S(1)}, u32[]{:S(2)}) copy-start(f32[128]{0:T(128)S(1)} %get-tuple-element.41) | copy-start | bytes 1540
  22.1 128.7 %copy-start.19 = (f32[128]{0:T(128)}, f32[128]{0:T(128)S(1)}, u32[]{:S(2)}) copy-start(f32[128]{0:T(128)S(1)} %get-tuple-element.42) | copy-start | bytes 1540
  22.2 128.7 %copy-start.21 = (f32[128]{0:T(128)}, f32[128]{0:T(128)S(1)}, u32[]{:S(2)}) copy-start(f32[128]{0:T(128)S(1)} %get-tuple-element.43) | copy-start | bytes 1540
  23.1 127.7 %collective-permute-start.3 = (bf16[3,1,128,128]{2,3,1,0:T(8,128)(2,1)S(1)}, bf16[3,1,128,128]{2,3,1,0:T(8,128)(2,1)S(1)}, u32[]{:S(2)}, u32[]{:S(2)}) collective-permute-start(bf16[3,1,128,128]{2,3,1,0:T(8,128)(2,1)S(1)} %get-tuple-element.24), channel_id=1, source_target_pairs={{1,0},{2,1},{3,2},{4,3},{5,4},{6,5},{7,6},{8,7},{9,8},{10,9},{11,1... | collective-permute-start | bytes 294920 | tf_op jit(solution)/shard_map/ppermute | solution.py:17
  24.4 126.4 %collective-permute-start.2 = (bf16[3,1,128,128]{2,3,1,0:T(8,128)(2,1)S(1)}, bf16[3,1,128,128]{2,3,1,0:T(8,128)(2,1)S(1)}, u32[]{:S(2)}, u32[]{:S(2)}) collective-permute-start(bf16[3,1,128,128]{2,3,1,0:T(8,128)(2,1)S(1)} %get-tuple-element.25), channel_id=1, source_target_pairs={{0,1},{1,2},{2,3},{3,4},{4,5},{5,6},{6,7},{7,8},{8,9},{9,10},{10,1... | collective-permute-start | bytes 294920 | tf_op jit(solution)/shard_map/ppermute | solution.py:14
  150.8 1.7 copy-start.3
  152.8 14.5 %copy-start = (bf16[1,8,128,128]{3,2,1,0:T(8,128)(2,1)S(1)}, bf16[1,8,128,128]{3,2,1,0:T(8,128)(2,1)}, u32[]{:S(2)}) copy-start(bf16[1,8,128,128]{3,2,1,0:T(8,128)(2,1)} %param.5) | copy-start | bytes 786436
  155.5 115.4 %collective-permute-start.5 = (bf16[1,8,128,128]{2,3,1,0:T(8,128)(2,1)S(1)}, bf16[1,8,128,128]{2,3,1,0:T(8,128)(2,1)}, u32[]{:S(2)}, u32[]{:S(2)}) collective-permute-start(bf16[1,8,128,128]{2,3,1,0:T(8,128)(2,1)S(1)} %bitcast.129), channel_id=1, source_target_pairs={{64,0},{128,64},{192,128},{256,192},{320,256},{384,320},{448,384},... | collective-permute-start | bytes 786440 | tf_op jit(solution)/shard_map/ppermute | solution.py:17
  161.9 109.0 %collective-permute-start.4 = (bf16[1,8,128,128]{2,3,1,0:T(8,128)(2,1)S(1)}, bf16[1,8,128,128]{2,3,1,0:T(8,128)(2,1)}, u32[]{:S(2)}, u32[]{:S(2)}) collective-permute-start(bf16[1,8,128,128]{2,3,1,0:T(8,128)(2,1)S(1)} %bitcast.130), channel_id=1, source_target_pairs={{0,64},{64,128},{128,192},{192,256},{256,320},{320,384},{384,448},... | collective-permute-start | bytes 786440 | tf_op jit(solution)/shard_map/ppermute | solution.py:14
  169.6 3.3 copy-start.24
  169.6 3.3 copy-start.26
  169.6 109.2 %copy-start.6 = (f32[128]{0:T(128)S(1)}, f32[128]{0:T(128)}, u32[]{:S(2)}) copy-start(f32[128]{0:T(128)} %copy-done.5) | copy-start | bytes 1540
  169.6 109.2 %copy-start.8 = (f32[128]{0:T(128)S(1)}, f32[128]{0:T(128)}, u32[]{:S(2)}) copy-start(f32[128]{0:T(128)} %copy-done.7) | copy-start | bytes 1540
  169.6 109.2 %copy-start.10 = (f32[128]{0:T(128)S(1)}, f32[128]{0:T(128)}, u32[]{:S(2)}) copy-start(f32[128]{0:T(128)} %copy-done.9) | copy-start | bytes 1540
  169.6 109.2 %copy-start.12 = (f32[128]{0:T(128)S(1)}, f32[128]{0:T(128)}, u32[]{:S(2)}) copy-start(f32[128]{0:T(128)} %copy-done.11) | copy-start | bytes 1540
  169.7 109.2 %copy-start.14 = (f32[128]{0:T(128)S(1)}, f32[128]{0:T(128)}, u32[]{:S(2)}) copy-start(f32[128]{0:T(128)} %copy-done.13) | copy-start | bytes 1540
  169.7 109.2 %copy-start.16 = (f32[128]{0:T(128)S(1)}, f32[128]{0:T(128)}, u32[]{:S(2)}) copy-start(f32[128]{0:T(128)} %copy-done.15) | copy-start | bytes 1540
  169.7 109.2 %copy-start.18 = (f32[128]{0:T(128)S(1)}, f32[128]{0:T(128)}, u32[]{:S(2)}) copy-start(f32[128]{0:T(128)} %copy-done.17) | copy-start | bytes 1540
  169.7 109.2 %copy-start.20 = (f32[128]{0:T(128)S(1)}, f32[128]{0:T(128)}, u32[]{:S(2)}) copy-start(f32[128]{0:T(128)} %copy-done.19) | copy-start | bytes 1540
  169.7 109.2 %copy-start.22 = (f32[128]{0:T(128)S(1)}, f32[128]{0:T(128)}, u32[]{:S(2)}) copy-start(f32[128]{0:T(128)} %copy-done.21) | copy-start | bytes 1540
  271.8 5.8 collective-permute-start.6
  273.1 5.8 collective-permute-start.7
  (5 other events, 6.4 us)
Sparse Core Ops, SparseCore 0:
  12.6 135.0 all-gather.2
  155.6 400.1 reduce-scatter.1
